TPU v7x, 256 devices: a whole 4x4x8 slice. The times are simulated.
256 devices in a mesh: expert: 64 (over z, y, core), mp: 4 (over x).
Axes of the slice: x: 4, y: 4, z: 8, core: 2. Of those that a mesh axis runs over, the one named last changes fastest.
Arguments:
- tokens: bfloat16 [16384, 2048], P('expert'), may hold values from -6 to 6
- out_grad: bfloat16 [16384, 2048], P('expert'), may hold values from -6 to 6
- expert_ids: int32 [16384, 1], P('expert'), may hold values from 0 to 31; in each aligned block of 256 rows (0 to 255, 256 to 511, ...) at most 16 rows name the same one
- w_in: bfloat16 [64, 2048, 2560], P('expert', None, 'mp'), may hold values from -0.125 to 0.125
- w_out: bfloat16 [64, 2560, 2048], P('expert', 'mp'), may hold values from -0.078125 to 0.078125
- in_row_mom: float32 [64, 1024], P('expert'), may hold values from 0.2 to 5
- in_col_mom: float32 [64, 2560], P('expert', 'mp'), may hold values from 0.2 to 5
- out_row_mom: float32 [64, 2560], P('expert', 'mp'), may hold values from 0.2 to 5
- out_col_mom: float32 [64, 1024], P('expert'), may hold values from 0.2 to 5
Outputs:
- token_grad: bfloat16 [16384, 2048], P('expert', 'mp')
- w_in_new: bfloat16 [64, 2048, 2560], P('expert', None, 'mp')
- w_out_new: bfloat16 [64, 2560, 2048], P('expert', 'mp')
- in_row_new: float32 [64, 1024], P('expert')
- in_col_new: float32 [64, 2560], P('expert', 'mp')
- out_row_new: float32 [64, 2560], P('expert', 'mp')
- out_col_new: float32 [64, 1024], P('expert')
Inputs may be any that keep to these rules, and one draw needn't show every extreme that they name: `expert_ids`: in the 256 tokens of one index of the expert axis (aligned blocks of rows) no expert is named more than 16 times, a bound that some block reaches.
All inputs are finite; a program needn't handle non-finite values.
Results may differ from a plain program's by a relative error of at most 0.0045.
The roundings to bfloat16 on the way count: a program that leaves them out, or rounds other values in their place, can miss the bound.
Values may be sent and summed in bfloat16 or wider, within the bound.
A program may use at most 128 MiB of HBM per device.

v0:
```python
import jax
import jax.numpy as jnp
from jax import lax
from jax.sharding import PartitionSpec as P

beta_two = 0.8
step_size = 0.01
epsilon_one = 1e-30


def partner(block, axis, apart):
    count = lax.axis_size(axis)
    route = []
    for low in range(count):
        high = low | 1 << apart
        if high != low and high < count:
            route += [(low, high), (high, low)]
    return lax.ppermute(block, axis, route)


def gelu_pair(preact, upstream):
    active, pull = jax.vjp(jax.nn.gelu, preact)
    return (active, pull(upstream)[0])


def spread_half(half_vector, half_index, full_width):
    zeroed = jnp.zeros((full_width,), jnp.float32)
    return lax.dynamic_update_slice(zeroed, half_vector, (half_index * (full_width // 2),))


def shards(
    tokens, out_grad, expert_ids, w_in, w_out, in_row_mom, in_col_mom, out_row_mom, out_col_mom
):
    tok_count, model_width = tokens.shape
    expert_count = lax.axis_size("expert")
    model_count = lax.axis_size("mp")
    pair_count = expert_count // 2
    capacity = 2 * tok_count // pair_count
    slot_total = pair_count * capacity
    position = lax.axis_index("expert")
    my_half = position % 2
    my_model = lax.axis_index("mp")
    w_local = w_in[0]
    v_local = w_out[0]
    hidden = w_local.shape[1]
    full_hidden = hidden * 2 * model_count
    half_width = model_width // 2
    chosen = expert_ids[:, 0]
    onehot = (chosen[:, None] == jnp.arange(pair_count, dtype=jnp.int32)[None, :]).astype(jnp.int32)
    earlier = jnp.cumsum(onehot, axis=0) - onehot
    slot_index = chosen * capacity + jnp.sum(earlier * onehot, axis=1)
    source = (
        jnp.full((slot_total,), tok_count, jnp.int32)
        .at[slot_index]
        .set(jnp.arange(tok_count, dtype=jnp.int32))
    )

    def pack_rows(values):
        picked = jnp.take(values, source, axis=0, mode="fill", fill_value=0)
        columns = picked.shape[1]
        doubled = jnp.broadcast_to(
            picked.reshape(pair_count, 1, capacity, columns), (pair_count, 2, capacity, columns)
        )
        return doubled.reshape(expert_count, capacity, columns)

    arrived_tokens, arrived_grads = (
        lax.all_to_all(pack_rows(tokens), "expert", split_axis=0, concat_axis=0, tiled=True),
        lax.all_to_all(pack_rows(out_grad), "expert", split_axis=0, concat_axis=0, tiled=True),
    )
    expert_tokens = arrived_tokens.reshape(expert_count * capacity, model_width)
    expert_grads = arrived_grads.reshape(expert_count * capacity, model_width)
    preact = jnp.dot(expert_tokens, w_local, preferred_element_type=jnp.float32)
    upstream = lax.dot_general(
        expert_grads, v_local, (((1,), (1,)), ((), ())), preferred_element_type=jnp.float32
    )
    active, pre_grad = gelu_pair(preact, upstream)
    active = active.astype(jnp.bfloat16)
    pre_grad = pre_grad.astype(jnp.bfloat16)
    gradient_in = lax.dot_general(
        expert_tokens, pre_grad, (((0,), (0,)), ((), ())), preferred_element_type=jnp.float32
    )
    gradient_out = lax.dot_general(
        active, expert_grads, (((0,), (0,)), ((), ())), preferred_element_type=jnp.float32
    )
    partial_grad = lax.psum_scatter(
        lax.dot_general(
            w_local, pre_grad, (((1,), (1,)), ((), ())), preferred_element_type=jnp.float32
        ),
        "mp",
        scatter_dimension=0,
        tiled=True,
    )
    feature_rows = partial_grad.shape[0]
    returned = lax.all_to_all(
        partial_grad.reshape(feature_rows, expert_count, capacity),
        "expert",
        split_axis=1,
        concat_axis=1,
        tiled=True,
    )
    paired = jnp.sum(returned.reshape(feature_rows, pair_count, 2, capacity), axis=2).reshape(
        feature_rows, slot_total
    )
    token_grad = jnp.take(paired, slot_index, axis=1).T.astype(jnp.bfloat16)
    leader = (my_model == 0).astype(jnp.float32)
    old_in_row = spread_half(in_row_mom[0], my_half, model_width) * leader
    old_out_column = spread_half(out_col_mom[0], my_half, model_width) * leader
    param_total = 2.0 * pair_count * model_width * full_hidden
    norm_part = jnp.sum(gradient_in * gradient_in) + jnp.sum(gradient_out * gradient_out)
    norm_total = lax.psum(norm_part, ("expert", "mp"))
    clip_factor = jnp.minimum(1.0, jnp.sqrt(param_total / norm_total))
    scaled_in = clip_factor * gradient_in
    scaled_out = clip_factor * gradient_out
    square_in = scaled_in * scaled_in
    square_out = scaled_out * scaled_out
    row_stat_out = jnp.mean(square_out, axis=1)
    stat_table = jnp.stack(
        [jnp.sum(square_in, axis=1), jnp.sum(square_out, axis=0), old_in_row, old_out_column]
    )
    totals = jnp.stack([jnp.sum(out_row_mom[0]), jnp.sum(row_stat_out)])
    row_stat_out, stat_table, totals = (row_stat_out, stat_table, totals)
    half_table, half_totals = lax.psum((stat_table, totals), "mp")
    other_table, other_totals = (
        partner(half_table.astype(jnp.bfloat16), "expert", 0).astype(half_table.dtype),
        partner(half_totals.astype(jnp.bfloat16), "expert", 0).astype(half_totals.dtype),
    )
    own_stats = half_table + other_table
    own_totals = half_totals + other_totals
    factor = 1.0
    row_factor_in = beta_two * own_stats[2] + (1.0 - beta_two) * (
        factor * own_stats[0] / full_hidden + epsilon_one
    )
    column_factor_in = beta_two * in_col_mom[0] + (1.0 - beta_two) * (
        factor * jnp.mean(square_in, axis=0) + epsilon_one
    )
    second_in = row_factor_in[:, None] * column_factor_in[None, :] / jnp.mean(row_factor_in)
    new_in = (
        w_local.astype(jnp.float32) - step_size * clip_factor * gradient_in * lax.rsqrt(second_in)
    ).astype(jnp.bfloat16)
    row_factor_out = beta_two * out_row_mom[0] + (1.0 - beta_two) * (
        factor * row_stat_out + epsilon_one
    )
    column_factor_out = beta_two * own_stats[3] + (1.0 - beta_two) * (
        factor * own_stats[1] / full_hidden + epsilon_one
    )
    mean_row_out = beta_two * own_totals[0] / full_hidden + (1.0 - beta_two) * (
        factor * own_totals[1] / full_hidden + epsilon_one
    )
    second_out = row_factor_out[:, None] * column_factor_out[None, :] / mean_row_out
    new_out = (
        v_local.astype(jnp.float32) - step_size * clip_factor * gradient_out * lax.rsqrt(second_out)
    ).astype(jnp.bfloat16)
    in_row_new = lax.dynamic_slice_in_dim(row_factor_in, my_half * half_width, half_width, 0)[None]
    out_col_new = lax.dynamic_slice_in_dim(column_factor_out, my_half * half_width, half_width, 0)[
        None
    ]
    return (
        token_grad,
        new_in[None],
        new_out[None],
        in_row_new,
        column_factor_in[None],
        row_factor_out[None],
        out_col_new,
    )


def solution(mesh):
    placed = (
        P("expert", None),
        P("expert", None),
        P("expert", None),
        P("expert", None, "mp"),
        P("expert", "mp", None),
        P("expert", None),
        P("expert", "mp"),
        P("expert", "mp"),
        P("expert", None),
    )
    return jax.shard_map(
        shards,
        mesh=mesh,
        in_specs=placed,
        out_specs=(
            P("expert", "mp"),
            P("expert", None, "mp"),
            P("expert", "mp", None),
            P("expert", None),
            P("expert", "mp"),
            P("expert", "mp"),
            P("expert", None),
        ),
        check_vma=False,
    )
```

profile of v0, /device:TPU:8, one launch (start us, length us, event | category | flops | bytes accessed | tf_op | source)
XLA Modules:
  0.0 418.0 jit_solution(13748377389985934341)
XLA Ops:
  7.2 0.8 fusion.28
  8.8 0.8 fusion.27
  9.5 0.7 and_reduce_fusion
  10.2 1.4 scatter_custom_fusion
  11.7 3.3 gather_fusion.2
  15.0 3.3 gather_fusion.1
  18.3 2.6 broadcast_select_fusion.1
  21.4 108.2 %all_to_all.15 = bf16[64,16,2048]{2,1,0:T(8,128)(2,1)} all-to-all(bf16[64,16,2048]{2,1,0:T(8,128)(2,1)S(1)} %bitcast.76), channel_id=1, replica_groups=mesh['expert'=64,'mp'=4] {'expert'}, dimensions={0} | all-to-all | bytes 8388608 | tf_op jit(solution)/shard_map/all_to_all | solution.py:67
  129.6 2.5 broadcast_in_dim.55
  132.1 5.6 %all-to-all-start = ((bf16[64,16,2048]{2,1,0:T(8,128)(2,1)}), bf16[64,16,2048]{2,1,0:T(8,128)(2,1)}, u32[]{:S(2)}, u32[]{:S(2)}) async-start(bf16[64,16,2048]{2,1,0:T(8,128)(2,1)} %bitcast.75), calls=%async_computation | async-start | bytes 8388608 | tf_op jit(solution)/shard_map/all_to_all | solution.py:68
  137.9 7.9 %fusion.12 = f32[1024,640]{1,0:T(8,128)} fusion(bf16[1024,2048]{1,0:T(8,128)(2,1)} %bitcast.80, bf16[1,2048,640]{2,1,0:T(8,128)(2,1)} %param.14), kind=kOutput, calls=%fused_computation.25 | convolution fusion | flops 2684354560 | bytes 9437184 | tf_op jit(solution)/shard_map/dot_general | solution.py:72
  145.8 88.0 %all-to-all-done = bf16[64,16,2048]{2,1,0:T(8,128)(2,1)} async-done(((bf16[64,16,2048]{2,1,0:T(8,128)(2,1)}), bf16[64,16,2048]{2,1,0:T(8,128)(2,1)}, u32[]{:S(2)}, u32[]{:S(2)}) %all-to-all-start) | async-done | bytes 4194336 | tf_op jit(solution)/shard_map/all_to_all | solution.py:68
  233.9 8.4 %fusion.10 = bf16[1024,640]{1,0:T(8,128)(2,1)S(1)} fusion(f32[1024,640]{1,0:T(8,128)} %fusion.12, bf16[1024,2048]{1,0:T(8,128)(2,1)} %bitcast.7, bf16[1,640,2048]{2,1,0:T(8,128)(2,1)} %param.15), kind=kOutput, calls=%fused_computation.23 | convolution fusion | flops 2697461760 | bytes 10747904 | tf_op jit(solution)/shard_map/dot_general | solution.py:73
  242.3 5.9 %convolution_bitcast_fusion = f32[2048,1024]{0,1:T(8,128)} fusion(bf16[1024,640]{1,0:T(8,128)(2,1)S(1)} %fusion.10, bf16[1,2048,640]{2,1,0:T(8,128)(2,1)S(1)} %copy-done.2), kind=kOutput, calls=%fused_computation.14 | convolution fusion | flops 2684354560 | bytes 12320768 | tf_op jit(solution)/shard_map/dot_general | solution.py:86
  248.2 0.6 copy-done.5
  249.3 0.6 multiply_reduce_fusion.3
  250.0 8.9 %multiply_reduce_fusion.1 = (f32[]{:T(128)}, f32[2048,640]{1,0:T(8,128)}) fusion(bf16[1024,2048]{1,0:T(8,128)(2,1)} %bitcast.81, bf16[1024,640]{1,0:T(8,128)(2,1)S(1)} %fusion.10), kind=kOutput, calls=%fused_computation.9 | convolution fusion | flops 2686976000 | bytes 10747908 | tf_op jit(solution)/shard_map/dot_general | solution.py:79
  258.8 8.2 %multiply_reduce_fusion = (f32[]{:T(128)}, f32[640,2048]{1,0:T(8,128)}) fusion(bf16[1024,2048]{1,0:T(8,128)(2,1)} %bitcast.7, f32[1024,640]{1,0:T(8,128)S(1)} %copy-done.8), kind=kOutput, calls=%fused_computation.8 | convolution fusion | flops 2692874240 | bytes 12058628 | tf_op jit(solution)/shard_map/dot_general | solution.py:82
  268.4 75.5 %psum.21 = f32[]{:T(128)} all-reduce(f32[]{:T(128)S(6)} %add.140), channel_id=1, replica_groups=mesh['expert'=64,'mp'=4] {'expert','mp'}, use_global_device_ids=true, to_apply=%region_8.10 | all-reduce | flops 1 | bytes 8 | tf_op jit(solution)/shard_map/psum | solution.py:110
  344.6 3.2 fusion.2
  347.9 8.2 %all-to-all-start.2 = ((f32[512,64,16]{0,2,1:T(8,128)}), f32[512,64,16]{0,2,1:T(8,128)}, u32[]{:S(2)}, u32[]{:S(2)}) async-start(f32[512,64,16]{0,2,1:T(8,128)} %bitcast.82), calls=%async_computation.3 | async-start | bytes 4194304 | tf_op jit(solution)/shard_map/all_to_all | solution.py:94
  356.7 1.4 pad_maximum_fusion.1
  358.1 3.3 fusion
  361.4 15.7 %all-reduce = (f32[4,2048]{1,0:T(4,128)S(1)}, f32[2]{0:T(128)S(1)}) all-reduce(f32[4,2048]{1,0:T(4,128)S(1)} %pad_maximum_fusion, f32[2]{0:T(128)S(1)} %pad_maximum_fusion.1), channel_id=1, replica_groups=mesh['expert'=64,'mp'=4] {'mp'}, use_global_device_ids=true, to_apply=%region_11.13 | all-reduce | flops 8194 | bytes 65552 | tf_op jit(solution)/shard_map/psum | solution.py:122
  380.3 0.6 fusion.43
  382.2 5.2 %fusion.16 = bf16[1,2048,640]{2,1,0:T(8,128)(2,1)} fusion(f32[]{:T(128)S(6)} %div.39, f32[640]{0:T(1024)S(1)} %get-tuple-element.16, f32[2048]{0:T(1024)S(1)} %bitcast.84, f32[2048,640]{1,0:T(8,128)} %get-tuple-element.31, f32[]{:T(128)S(6)} %mul.243, bf16[1,2048,640]{2,1,0:T(8,128)(2,1)} %param.14), kind=kLoop, calls=%fused_computation.30 | loop fusion | flops 9175040 | bytes 10496520 | tf_op jit(solution)/shard_map/broadcast_in_dim | solution.py:159
  388.0 0.8 copy-done.3
  388.8 2.8 fusion.17
  391.6 15.7 %all-to-all-done.2 = f32[512,64,16]{0,2,1:T(8,128)} async-done(((f32[512,64,16]{0,2,1:T(8,128)}), f32[512,64,16]{0,2,1:T(8,128)}, u32[]{:S(2)}, u32[]{:S(2)}) %all-to-all-start.2) | async-done | bytes 2097184 | tf_op jit(solution)/shard_map/all_to_all | solution.py:94
  407.3 1.9 bitcast_reduce_fusion
  409.1 1.2 gather_fusion
  410.3 0.8 select_convert_fusion
  (54 shorter events, 5.8 us)
Async XLA Ops:
  7.2 4.5 %copy-start = (bf16[256,2048]{1,0:T(8,128)(2,1)S(1)}, bf16[256,2048]{1,0:T(8,128)(2,1)}, u32[]{:S(2)}) copy-start(bf16[256,2048]{1,0:T(8,128)(2,1)} %param.11) | copy-start | bytes 3145732
  11.7 3.3 copy-start.1
  132.1 101.8 %all-to-all-start = ((bf16[64,16,2048]{2,1,0:T(8,128)(2,1)}), bf16[64,16,2048]{2,1,0:T(8,128)(2,1)}, u32[]{:S(2)}, u32[]{:S(2)}) async-start(bf16[64,16,2048]{2,1,0:T(8,128)(2,1)} %bitcast.75), calls=%async_computation | async-start | bytes 8388608 | tf_op jit(solution)/shard_map/all_to_all | solution.py:68
  137.7 210.2 %reduce-scatter.2.cloned.1.call-start = ((), (), s32[]{:S(2)}) async-start(), calls=%async_computation.4 | async-start | bytes 10485760 | tf_op jit(solution)/shard_map/reduce_scatter | solution.py:85
  233.9 8.4 %copy-start.2 = (bf16[1,2048,640]{2,1,0:T(8,128)(2,1)S(1)}, bf16[1,2048,640]{2,1,0:T(8,128)(2,1)}, u32[]{:S(2)}) copy-start(bf16[1,2048,640]{2,1,0:T(8,128)(2,1)} %param.14) | copy-start | bytes 7864324
  248.2 0.7 copy-start.5
  248.2 0.9 copy-start.6
  248.2 1.2 copy-start.4
  250.0 8.9 %copy-start.8 = (f32[1024,640]{1,0:T(8,128)S(1)}, f32[1024,640]{1,0:T(8,128)}, u32[]{:S(2)}) copy-start(f32[1024,640]{1,0:T(8,128)} %fusion.12) | copy-start | bytes 7864324
  347.9 59.4 %all-to-all-start.2 = ((f32[512,64,16]{0,2,1:T(8,128)}), f32[512,64,16]{0,2,1:T(8,128)}, u32[]{:S(2)}, u32[]{:S(2)}) async-start(f32[512,64,16]{0,2,1:T(8,128)} %bitcast.82), calls=%async_computation.3 | async-start | bytes 4194304 | tf_op jit(solution)/shard_map/all_to_all | solution.py:94
  358.1 19.7 %copy-start.7 = (f32[1,640]{1,0:T(1,128)S(1)}, f32[1,640]{1,0:T(1,128)}, u32[]{:S(2)}) copy-start(f32[1,640]{1,0:T(1,128)} %param.17) | copy-start | bytes 7684
  377.1 1.3 collective-permute-start.1
  377.2 3.1 collective-permute-start
  382.2 5.2 %slice-start = ((s8[5242880]{0:T(1024)(128)(4,1)}), s8[4194304]{0:T(1024)(128)(4,1)S(1)}, s32[]{:S(2)}) async-start(s8[5242880]{0:T(1024)(128)(4,1)} %bitcast.73), calls=%async_computation.5 | async-start | bytes 8388608
  382.2 5.7 %slice-start.1 = ((s8[5242880]{0:T(1024)(128)(4,1)}), s8[1048576]{0:T(1024)(128)(4,1)S(1)}, s32[]{:S(2)}) async-start(s8[5242880]{0:T(1024)(128)(4,1)} %bitcast.73), calls=%async_computation.6 | async-start | bytes 2097152
  382.2 6.6 %copy-start.3 = (bf16[1,640,2048]{2,1,0:T(8,128)(2,1)S(1)}, bf16[1,640,2048]{2,1,0:T(8,128)(2,1)}, u32[]{:S(2)}) copy-start(bf16[1,640,2048]{2,1,0:T(8,128)(2,1)} %param.15) | copy-start | bytes 7864324
Sparse Core Ops, SparseCore 0:
  248.3 80.1 reduce-scatter.1
where the time goes:
time: 419 us; the launch traced here: 418 us
  blocking collectives  199 us (47%)
  waiting for transfers between devices  104 us (25%)
  matrix products  39.3 us (9%)
  other arithmetic  26.5 us (6%)
  between operations  18.3 us (4%)
  local copies, waits for them, and re-layouts  16 us (4%)
  starting transfers between devices  14.7 us (4%)
    all_to_all x1, blocking collectives, shards(): lax.all_to_all(pack_rows(tokens), 'expert', split_axis=0, concat_axis=0,...  108 us
    all_to_all x1, waiting for transfers between devices, shards(): lax.all_to_all(pack_rows(out_grad), 'expert', split_axis=0, concat_axis=0...  88 us
    psum x1, blocking collectives, shards(): norm_total = lax.psum(norm_part, ('expert', 'mp'))  75.5 us
    all_to_all x1, waiting for transfers between devices, shards(): lax.all_to_all(partial_grad.reshape(feature_rows, expert_count, capacity)...  15.7 us
    psum x1, blocking collectives, shards(): half_table, half_totals = lax.psum((stat_table, totals), 'mp')  15.7 us
    dot_general x1, matrix products, shards(): lax.dot_general(expert_tokens, pre_grad, (((0,), (0,)), ((), ())), prefer...  8.87 us
    dot_general x1, matrix products, shards(): lax.dot_general(expert_grads, v_local, (((1,), (1,)), ((), ())), preferre...  8.43 us
  transfers between devices with their start and end apart: 5, of which 2 were waited for; matrix products, arithmetic and copies ran while one was open for 11% of the time, Pallas kernels for 0%

commit v1 on v0

v1 whole, which is shorter than its diff:
```python
import functools

import jax
import jax.numpy as jnp
from jax import lax
from jax.experimental import pallas as pl
from jax.experimental.pallas import tpu as pltpu
from jax.sharding import PartitionSpec as P

MESH = pl.DeviceIdType.MESH
F32 = jnp.float32
BF16 = jnp.bfloat16
CHIPS_Y = 4
CAP = 16
beta_two = 0.8
step_size = 0.01
epsilon_one = 1e-30
root_two_over_pi = 0.7978845608028654


def dot(left, right, contract):
    return lax.dot_general(left, right, (contract, ((), ())), preferred_element_type=F32)


def kernel(
    sizes,
    tok_hbm, grad_hbm, ids_ref, w_hbm, v_hbm, irm_ref, icm_ref, orm_ref, ocm_ref,
    tg_ref, wn_hbm, vn_hbm, irn_ref, icn_ref, orn_ref, ocn_ref,
    tokq, gradq, place, packed, buf, w_v, v_v, g_in, g_out, pre_s, up_s, act_s, pg_s,
    tkeep, tsend, trecv, sown, d2s, d2r, nbs, nbr, fin, rbuf, pbuf, nbuf, rs_in, rs_out, a_in, a_out,
    load_sem, a2a_ss, a2a_rs, x1_ss, x1_rs, x2_ss, x2_rs, cf_ss, cf_rs, tc_ss, tc_rs,
    d2_ss, d2_rs, nb_ss, nb_rs, ret_ss, ret_rs, st1_ss, st1_rs, st2_ss, st2_rs, out_sem,
):
    T, D, H, Z, Y = sizes
    K = Z * Y
    NCH = Z // 2
    DQ, DH = D // 4, D // 2
    RG = Y * CAP
    RK = 2 * RG
    R = 2 * RK
    FF = 8 * H
    e = lax.axis_index("expert")
    x = lax.axis_index("mp")
    k = e // 2
    c = e % 2
    z = k // Y
    y = k % Y
    xr, xo, xl = (x + 1) % 4, (x + 2) % 4, (x + 3) % 4
    quarter = (x, xr, xo, xl)
    right, left, core = (e, xr), (e, xl), (2 * k + 1 - c, x)

    def remote(src, dst, ss, rs, dev):
        return pltpu.make_async_remote_copy(
            src_ref=src, dst_ref=dst, send_sem=ss, recv_sem=rs, device_id=dev, device_id_type=MESH
        )

    def expert_at(dz, dy):
        return ((z + dz + Z) % Z) * Y + (y + dy + Y) % Y

    def dz_of(ch, jj):
        return -ch if jj == 0 else ch + 1

    def rows(cr, jj):
        return pl.ds(cr * RK + jj * RG, RG)

    def slots(expert):
        return pl.ds(pl.multiple_of(expert * CAP, CAP), CAP)

    def a2a(ch, jj, dy):
        to = expert_at(dz_of(ch, jj), dy)
        return remote(
            packed.at[:, slots(to), :],
            buf.at[x, ch, :, pl.ds(jj * RG + dy * CAP, CAP), :],
            a2a_ss.at[2 * ch + jj, dy], a2a_rs.at[2 * ch + jj, dy], (2 * to + c, x),
        )

    def x1(ch, jj, way, q):
        here = buf.at[q, ch, :, rows(0, jj), :]
        return remote(
            here, here, x1_ss.at[2 * ch + jj, way], x1_rs.at[2 * ch + jj, way], (right, left)[way]
        )

    def x2(ch, jj, way, q):
        here = buf.at[q, ch, way, rows(0, jj), :]
        return remote(
            here, here, x2_ss.at[2 * ch + jj, way], x2_rs.at[2 * ch + jj, way], (right, left)[way]
        )

    def cf(ch, jj, rq):
        return remote(
            buf.at[quarter[rq], ch, :, rows(0, jj), :],
            buf.at[quarter[rq], ch, :, rows(1, jj), :],
            cf_ss.at[2 * ch + jj, rq], cf_rs.at[2 * ch + jj, rq], core,
        )

    def tc(ch):
        return remote(tsend.at[ch], trecv.at[ch], tc_ss.at[ch], tc_rs.at[ch], core)

    def d2(ch, way):
        return remote(
            d2s.at[ch, way], d2r.at[ch, way], d2_ss.at[ch, way], d2_rs.at[ch, way], (right, left)[way]
        )

    def nb(ch, way):
        return remote(
            nbs.at[ch, way], nbr.at[ch, way], nb_ss.at[ch, way], nb_rs.at[ch, way], (right, left)[way]
        )

    def ret(ch, jj, dy, landing):
        to = expert_at(-dz_of(ch, jj), -dy)
        return remote(
            fin.at[ch, pl.ds(jj * RG + dy * CAP, CAP), :],
            rbuf.at[slots(landing), :],
            ret_ss.at[2 * ch + jj, dy], ret_rs.at[2 * ch + jj, dy], (2 * to + c, x),
        )

    def st1(dx, dc, slot):
        to = (2 * k + (c + dc) % 2, (x + dx) % 4)
        return remote(
            pbuf.at[slot], pbuf.at[slot], st1_ss.at[dx, dc], st1_rs.at[dx, dc], to
        )

    def st2(off, slot):
        to = (2 * ((k + off) % K) + c, x)
        return remote(nbuf.at[slot], nbuf.at[slot], st2_ss.at[off], st2_rs.at[off], to)

    columns = pl.ds(pl.multiple_of(x * DQ, DQ), DQ)
    loads = [
        pltpu.make_async_copy(tok_hbm.at[:, columns], tokq, load_sem.at[0]),
        pltpu.make_async_copy(grad_hbm.at[:, columns], gradq, load_sem.at[1]),
        pltpu.make_async_copy(w_hbm.at[0], w_v, load_sem.at[2]),
        pltpu.make_async_copy(v_hbm.at[0], v_v, load_sem.at[3]),
    ]
    for load in loads:
        load.start()
    barrier = pltpu.get_barrier_semaphore()
    column_peers = [(dx, dc) for dx in range(4) for dc in range(2) if dx or dc]
    for off in range(1, K):
        pl.semaphore_signal(
            barrier, inc=1, device_id=(2 * ((k + off) % K) + c, x), device_id_type=MESH
        )
    for dx, dc in column_peers:
        pl.semaphore_signal(
            barrier, inc=1, device_id=(2 * k + (c + dc) % 2, (x + dx) % 4), device_id_type=MESH
        )

    lanes = max(128, K)
    chosen = ids_ref[...]
    onehot = jnp.where(lax.broadcasted_iota(jnp.int32, (T, lanes), 1) == chosen, 1.0, 0.0)
    below = jnp.where(
        lax.broadcasted_iota(jnp.int32, (T, T), 0) > lax.broadcasted_iota(jnp.int32, (T, T), 1), 1.0, 0.0
    )
    earlier = dot(below.astype(BF16), onehot.astype(BF16), ((1,), (0,)))
    rank = jnp.sum(earlier * onehot, axis=1, keepdims=True)
    slot = chosen * CAP + rank.astype(jnp.int32)
    place[...] = jnp.where(
        lax.broadcasted_iota(jnp.int32, (T, K * CAP), 1) == slot, 1.0, 0.0
    ).astype(BF16)
    loads[0].wait()
    packed[0] = dot(place[...], tokq[...], ((0,), (0,))).astype(BF16)
    loads[1].wait()
    packed[1] = dot(place[...], gradq[...], ((0,), (0,))).astype(BF16)
    pl.semaphore_wait(barrier, K - 1 + len(column_peers))

    every = [(ch, jj, dy) for ch in range(NCH) for jj in range(2) for dy in range(Y)][1:]
    for ch, jj, dy in every:
        a2a(ch, jj, dy).start()
    own = pltpu.make_async_copy(
        packed.at[:, slots(k), :], buf.at[x, 0, :, pl.ds(0, CAP), :], load_sem.at[4]
    )
    own.start()
    g_in[...] = jnp.zeros_like(g_in)
    g_out[...] = jnp.zeros_like(g_out)

    def step_a(ch, jj, first=False):
        for dy in range(Y):
            if first and dy == 0:
                own.wait()
            else:
                a2a(ch, jj, dy).wait_recv()
        x1(ch, jj, 0, x).start()
        x1(ch, jj, 1, x).start()
        cf(ch, jj, 0).start()

    def step_b(ch, jj):
        x1(ch, jj, 0, xl).wait_recv()
        x2(ch, jj, 0, xl).start()
        x1(ch, jj, 1, xr).wait_recv()
        x2(ch, jj, 1, xr).start()
        cf(ch, jj, 3).start()
        cf(ch, jj, 1).start()

    def step_c(ch, jj):
        x2(ch, jj, 0, xo).wait_recv()
        x2(ch, jj, 1, xo).wait_recv()
        cf(ch, jj, 2).start()

    def step_d(ch):
        for jj in range(2):
            for rq in range(4):
                cf(ch, jj, rq).wait_recv()

    def forward(ch):
        for q in range(4):
            part = slice(q * DQ, (q + 1) * DQ)
            pre = dot(buf[q, ch, 0], w_v[part, :], ((1,), (0,)))
            up = dot(buf[q, ch, 1], v_v[:, part], ((1,), (1,)))
            pre_s[...] = pre if q == 0 else pre_s[...] + pre
            up_s[...] = up if q == 0 else up_s[...] + up

        def activate(i, carry):
            some = pl.ds(pl.multiple_of(i * 32, 32), 32)
            p = pre_s[some, :]
            square = p * p
            tanh = jnp.tanh(root_two_over_pi * (p + 0.044715 * (p * square)))
            cdf = 0.5 * (1.0 + tanh)
            slope = cdf + (0.5 * root_two_over_pi) * p * (1.0 - tanh * tanh) * (
                1.0 + (3.0 * 0.044715) * square
            )
            act_s[some, :] = (p * cdf).astype(BF16)
            pg_s[some, :] = (up_s[some, :] * slope).astype(BF16)
            return carry

        lax.fori_loop(0, R // 32, activate, 0)
        for q in range(4):
            part = slice(q * DQ, (q + 1) * DQ)
            t = dot(pg_s[...], w_v[part, :], ((1,), (1,)))
            tsend[ch, q] = t[RK:].astype(BF16)
            tkeep[q] = t[:RK]
        tc(ch).start()

    def grads_in(ch):
        for q in range(4):
            part = slice(q * DQ, (q + 1) * DQ)
            g_in[part, :] += dot(buf[q, ch, 0], pg_s[...], ((0,), (0,)))

    def grads_out(ch):
        for q in range(4):
            part = slice(q * DQ, (q + 1) * DQ)
            g_out[:, part] += dot(act_s[...], buf[q, ch, 1], ((0,), (0,)))

    def step_r2(ch):
        tc(ch).wait_recv()
        both = tkeep[xo] + trecv[ch, xo].astype(F32)
        d2s[ch, 0] = both[:RG].astype(BF16)
        d2s[ch, 1] = both[RG:].astype(BF16)
        d2(ch, 0).start()
        d2(ch, 1).start()
        sown[ch] = tkeep[x] + trecv[ch, x].astype(F32)

    def step_r3(ch):
        d2(ch, 0).wait_recv()
        to_right = tkeep[xr] + trecv[ch, xr].astype(F32)
        nbs[ch, 0, :RG] = (to_right[:RG] + d2r[ch, 0].astype(F32)).astype(BF16)
        nbs[ch, 0, RG:] = to_right[RG:].astype(BF16)
        nb(ch, 0).start()
        d2(ch, 1).wait_recv()
        to_left = tkeep[xl] + trecv[ch, xl].astype(F32)
        nbs[ch, 1, :RG] = to_left[:RG].astype(BF16)
        nbs[ch, 1, RG:] = (to_left[RG:] + d2r[ch, 1].astype(F32)).astype(BF16)
        nb(ch, 1).start()

    def step_r4(ch):
        nb(ch, 0).wait_recv()
        nb(ch, 1).wait_recv()
        fin[ch] = (sown[ch] + nbr[ch, 0].astype(F32) + nbr[ch, 1].astype(F32)).astype(BF16)
        for jj in range(2):
            for dy in range(Y):
                if jj or dy:
                    ret(ch, jj, dy, k).start()

        @pl.when(ch > 0)
        def _():
            ret(ch, 0, 0, k).start()

        @pl.when(ch == 0)
        def _():
            rbuf[slots(k), :] = fin[0, :CAP, :]

    def also(condition, *steps):
        @pl.when(condition)
        def _():
            for function, *args in steps:
                function(*args)

    step_a(0, 0, first=True)
    step_a(0, 1)
    step_b(0, 0)
    step_a(1, 0)
    step_b(0, 1)
    step_c(0, 0)
    step_a(1, 1)
    step_b(1, 0)
    step_c(0, 1)
    loads[2].wait()
    loads[3].wait()

    def chunk(ch, carry):
        also(ch + 2 < NCH, (step_a, ch + 2, 0))
        also(ch + 1 < NCH, (step_b, ch + 1, 1), (step_c, ch + 1, 0))
        step_d(ch)
        forward(ch)
        also(ch > 0, (step_r4, ch - 1))
        also(ch + 2 < NCH, (step_a, ch + 2, 1), (step_b, ch + 2, 0))
        grads_in(ch)
        step_r2(ch)
        also(ch + 1 < NCH, (step_c, ch + 1, 1))
        grads_out(ch)
        step_r3(ch)
        return carry

    lax.fori_loop(0, NCH, chunk, 0)

    def squares_in(i, total):
        some = pl.ds(pl.multiple_of(i * 128, 128), 128)
        g = g_in[some, :]
        s = g * g
        narrow = s[:, :128]
        for t in range(1, H // 128):
            narrow = narrow + s[:, t * 128 : (t + 1) * 128]
        rs_in[:, some] = jnp.sum(narrow.T, axis=0, keepdims=True)
        return total + jnp.sum(s.reshape(16, 8, H), axis=0)

    def squares_out(i, total):
        some = pl.ds(pl.multiple_of(i * 128, 128), 128)
        g = g_out[some, :]
        s = g * g
        narrow = s[:, :128]
        for t in range(1, D // 128):
            narrow = narrow + s[:, t * 128 : (t + 1) * 128]
        rs_out[:, some] = jnp.sum(narrow.T, axis=0, keepdims=True)
        return total + jnp.sum(s.reshape(16, 8, D), axis=0)

    cs_in = jnp.sum(
        lax.fori_loop(0, D // 128, squares_in, jnp.zeros((8, H), F32)), axis=0, keepdims=True
    )
    cs_out = jnp.sum(
        lax.fori_loop(0, H // 128, squares_out, jnp.zeros((8, D), F32)), axis=0, keepdims=True
    )

    def total_of(row):
        return jnp.sum(row, axis=1, keepdims=True)

    mine = x * 2 + c
    norm_part = total_of(cs_in) + total_of(cs_out)
    pbuf[mine, 0:1] = rs_in[:, :DH]
    pbuf[mine, 1:2] = rs_in[:, DH:]
    pbuf[mine, 2:3] = cs_out[:, :DH]
    pbuf[mine, 3:4] = cs_out[:, DH:]
    pbuf[mine, 4:5] = irm_ref[...]
    pbuf[mine, 5:6] = ocm_ref[...]
    pbuf[mine, 6:7] = jnp.broadcast_to(norm_part, (1, DH))
    pbuf[mine, 7:8, : DH // 2] = jnp.broadcast_to(total_of(orm_ref[...]), (1, DH // 2))
    pbuf[mine, 7:8, DH // 2 :] = jnp.broadcast_to(total_of(rs_out[...]), (1, DH // 2))
    for dx, dc in column_peers:
        st1(dx, dc, mine).start()
    step_r4(NCH - 1)
    for dx, dc in column_peers:
        st1(dx, dc, ((x - dx + 4) % 4) * 2 + (c + dc) % 2).wait_recv()
    sums = pbuf[0]
    for s in range(1, 8):
        sums = sums + pbuf[s]
    nbuf[k] = jnp.broadcast_to(sums[6:7, :128], (8, 128))
    for off in range(1, K):
        st2(off, k).start()

    for ch, jj, dy in every:
        ret(ch, jj, dy, expert_at(dz_of(ch, jj), dy)).wait_recv()
    tg_ref[...] = dot(place[...], rbuf[...], ((1,), (0,))).astype(BF16)

    for off in range(1, K):
        st2(off, (k - off + K) % K).wait_recv()
    norm_total = jnp.sum(nbuf[...], axis=0)[0:1, 0:1]
    clip = jnp.minimum(1.0, jnp.sqrt((2.0 * K * D * FF) / norm_total))
    clip_two = clip * clip
    zero, one = pbuf[x * 2], pbuf[x * 2 + 1]
    old_in_row = jnp.concatenate([zero[4:5], one[4:5]], axis=1)
    old_out_col = jnp.concatenate([zero[5:6], one[5:6]], axis=1)
    row_in = jnp.concatenate([sums[0:1], sums[1:2]], axis=1)
    col_out = jnp.concatenate([sums[2:3], sums[3:4]], axis=1)

    def moved(old, squares, count):
        return beta_two * old + (1.0 - beta_two) * (clip_two * (squares / count) + epsilon_one)

    in_row = moved(old_in_row, row_in, FF)
    in_col = moved(icm_ref[...], cs_in, D)
    out_row = moved(orm_ref[...], rs_out[...], D)
    out_col = moved(old_out_col, col_out, FF)
    mean_in = total_of(in_row) / D
    mean_out = moved(sums[7:8, 0:1] / FF, sums[7:8, DH // 2 : DH // 2 + 1] / D, FF)
    irn_ref[...] = jnp.where(c == 0, in_row[:, :DH], in_row[:, DH:])
    ocn_ref[...] = jnp.where(c == 0, out_col[:, :DH], out_col[:, DH:])
    icn_ref[...] = in_col
    orn_ref[...] = out_row
    a_in[...] = (step_size * clip * jnp.sqrt(mean_in)) * lax.rsqrt(in_row)
    a_out[...] = (step_size * clip * jnp.sqrt(mean_out)) * lax.rsqrt(out_row)
    b_in = lax.rsqrt(in_col)
    b_out = lax.rsqrt(out_col)

    def update(weight, gradient, a, b, width):
        def block(i, carry):
            some = pl.ds(pl.multiple_of(i * 128, 128), 128)
            scale = jnp.broadcast_to(a[:, some], (128, 128)).T
            for t in range(width // 128):
                part = slice(t * 128, (t + 1) * 128)
                moved_by = gradient[some, part] * scale * b[:, part]
                weight[some, part] = (weight[some, part].astype(F32) - moved_by).astype(BF16)
            return carry

        return block

    outs = []
    update_in = update(w_v, g_in, a_in, b_in, H)
    for q in range(4):
        lax.fori_loop(q * DQ // 128, (q + 1) * DQ // 128, update_in, 0)
        part = pl.ds(q * DQ, DQ)
        outs.append(pltpu.make_async_copy(w_v.at[part, :], wn_hbm.at[0, part, :], out_sem.at[q]))
        outs[-1].start()
    update_out = update(v_v, g_out, a_out, b_out, D)
    for i in range(H // 128):
        update_out(i, 0)
        part = pl.ds(i * 128, 128)
        outs.append(pltpu.make_async_copy(v_v.at[part, :], vn_hbm.at[0, part, :], out_sem.at[4 + i]))
        outs[-1].start()

    for ch, jj, dy in every:
        a2a(ch, jj, dy).wait_send()
        ret(ch, jj, dy, k).wait_send()
    for ch in range(NCH):
        tc(ch).wait_send()
        for way in range(2):
            d2(ch, way).wait_send()
            nb(ch, way).wait_send()
            for jj in range(2):
                x1(ch, jj, way, x).wait_send()
                x2(ch, jj, way, (xl, xr)[way]).wait_send()
        for jj in range(2):
            for rq in range(4):
                cf(ch, jj, rq).wait_send()
    for dx, dc in column_peers:
        st1(dx, dc, mine).wait_send()
    for off in range(1, K):
        st2(off, k).wait_send()
    for out in outs:
        out.wait()


def shards(
    tokens, out_grad, expert_ids, w_in, w_out, in_row_mom, in_col_mom, out_row_mom, out_col_mom
):
    T, D = tokens.shape
    H = w_in.shape[2]
    K = lax.axis_size("expert") // 2
    Y = CHIPS_Y
    Z = K // Y
    NCH, DQ = Z // 2, D // 4
    RG = Y * CAP
    RK, R = 2 * RG, 4 * RG
    hbm = pl.BlockSpec(memory_space=pl.ANY)
    vmem = pl.BlockSpec(memory_space=pltpu.VMEM)
    dma = pltpu.SemaphoreType.DMA
    scratch = [
        pltpu.VMEM((T, DQ), BF16),
        pltpu.VMEM((T, DQ), BF16),
        pltpu.VMEM((T, K * CAP), BF16),
        pltpu.VMEM((2, K * CAP, DQ), BF16),
        pltpu.VMEM((4, NCH, 2, R, DQ), BF16),
        pltpu.VMEM((D, H), BF16),
        pltpu.VMEM((H, D), BF16),
        pltpu.VMEM((D, H), F32),
        pltpu.VMEM((H, D), F32),
        pltpu.VMEM((R, H), F32),
        pltpu.VMEM((R, H), F32),
        pltpu.VMEM((R, H), BF16),
        pltpu.VMEM((R, H), BF16),
        pltpu.VMEM((4, RK, DQ), F32),
        pltpu.VMEM((NCH, 4, RK, DQ), BF16),
        pltpu.VMEM((NCH, 4, RK, DQ), BF16),
        pltpu.VMEM((NCH, RK, DQ), F32),
        pltpu.VMEM((NCH, 2, RG, DQ), BF16),
        pltpu.VMEM((NCH, 2, RG, DQ), BF16),
        pltpu.VMEM((NCH, 2, RK, DQ), BF16),
        pltpu.VMEM((NCH, 2, RK, DQ), BF16),
        pltpu.VMEM((NCH, RK, DQ), BF16),
        pltpu.VMEM((K * CAP, DQ), BF16),
        pltpu.VMEM((8, 8, D // 2), F32),
        pltpu.VMEM((K, 8, 128), F32),
        pltpu.VMEM((1, D), F32),
        pltpu.VMEM((1, H), F32),
        pltpu.VMEM((1, D), F32),
        pltpu.VMEM((1, H), F32),
        dma((5,)),
        dma((Z, Y)), dma((Z, Y)),
        dma((Z, 2)), dma((Z, 2)),
        dma((Z, 2)), dma((Z, 2)),
        dma((Z, 4)), dma((Z, 4)),
        dma((NCH,)), dma((NCH,)),
        dma((NCH, 2)), dma((NCH, 2)),
        dma((NCH, 2)), dma((NCH, 2)),
        dma((Z, Y)), dma((Z, Y)),
        dma((4, 2)), dma((4, 2)),
        dma((K,)), dma((K,)),
        dma((4 + H // 128,)),
    ]
    return pl.pallas_call(
        functools.partial(kernel, (T, D, H, Z, Y)),
        out_shape=(
            jax.ShapeDtypeStruct((T, DQ), BF16),
            jax.ShapeDtypeStruct(w_in.shape, BF16),
            jax.ShapeDtypeStruct(w_out.shape, BF16),
            jax.ShapeDtypeStruct(in_row_mom.shape, F32),
            jax.ShapeDtypeStruct(in_col_mom.shape, F32),
            jax.ShapeDtypeStruct(out_row_mom.shape, F32),
            jax.ShapeDtypeStruct(out_col_mom.shape, F32),
        ),
        in_specs=[hbm, hbm, vmem, hbm, hbm, vmem, vmem, vmem, vmem],
        out_specs=(vmem, hbm, hbm, vmem, vmem, vmem, vmem),
        scratch_shapes=scratch,
        compiler_params=pltpu.CompilerParams(
            collective_id=0, has_side_effects=True, vmem_limit_bytes=56 * 1024 * 1024
        ),
    )(tokens, out_grad, expert_ids, w_in, w_out, in_row_mom, in_col_mom, out_row_mom, out_col_mom)


def solution(mesh):
    placed = (
        P("expert", None),
        P("expert", None),
        P("expert", None),
        P("expert", None, "mp"),
        P("expert", "mp", None),
        P("expert", None),
        P("expert", "mp"),
        P("expert", "mp"),
        P("expert", None),
    )
    return jax.shard_map(
        shards,
        mesh=mesh,
        in_specs=placed,
        out_specs=(
            P("expert", "mp"),
            P("expert", None, "mp"),
            P("expert", "mp", None),
            P("expert", None),
            P("expert", "mp"),
            P("expert", "mp"),
            P("expert", None),
        ),
        check_vma=False,
    )
```

time: 419 us -> 115 us (0.27)
  blocking collectives: 199 us -> 0 us
  waiting for transfers between devices: 104 us -> 0 us
  Pallas kernels: 0 us -> 102 us
  matrix products: 39.3 us -> 0 us
  other arithmetic: 26.5 us -> 0 us
  between operations: 18.3 us -> 0.66 us
  starting transfers between devices: 14.7 us -> 0 us
  local copies, waits for them, and re-layouts: 16 us -> 10.6 us
    all_to_all x1 -> x0, blocking collectives: 108 us -> none  [shards(): lax.all_to_all(pack_rows(tokens), 'expert', split_axis=0, concat_axis=0,...]
    all_to_all x2 -> x0, waiting for transfers between devices: 104 us -> none  [the longest x1 88 us: shards(): lax.all_to_all(pack_rows(out_grad), 'expert', split_axis=0, concat_axis=0...]
    pallas_call x0 -> x1, Pallas kernels: none -> 102 us  [shards(): pl.pallas_call(functools.partial(kernel, (T, D, H, Z, Y)), out_shape=(jax...]
    psum x2 -> x0, blocking collectives: 91.2 us -> none  [the longest x1 75.5 us: shards(): norm_total = lax.psum(norm_part, ('expert', 'mp'))]
    dot_general x5 -> x0, matrix products: 39.3 us -> none  [the longest x1 8.87 us: shards(): lax.dot_general(expert_tokens, pre_grad, (((0,), (0,)), ((), ())), prefer...]
    all_to_all x2 -> x0, starting transfers between devices: 13.9 us -> none  [the longest x1 8.23 us: shards(): lax.all_to_all(partial_grad.reshape(feature_rows, expert_count, capacity)...]
    reduce_sum x5 -> x0, other arithmetic: 9.8 us -> none  [the longest x1 3.26 us: shards(): jnp.mean(square_in, axis=0)]
    unnamed x22 -> x18, local copies, waits for them, and re-layouts: 2.07 us -> 10.6 us
  transfers between devices with their start and end apart: 5 -> 0, of which waited for: 2 -> 0; matrix products, arithmetic and copies ran while one was open for 11% -> 0% of each run, Pallas kernels for 0% -> 0%
where the time goes in v1:
time: 115 us; the launch traced here: 114 us
  Pallas kernels  102 us (89%)
  local copies, waits for them, and re-layouts  10.6 us (9%)
    pallas_call x1, Pallas kernels, shards(): pl.pallas_call(functools.partial(kernel, (T, D, H, Z, Y)), out_shape=(jax...  102 us
    unnamed x18, local copies, waits for them, and re-layouts  10.6 us

profile of v1, /device:TPU:8, one launch (start us, length us, event | category | flops | bytes accessed | tf_op | source)
XLA Modules:
  0.0 113.7 jit_solution(125315028304550653)
XLA Ops:
  0.6 1.5 %copy.16.ids_ref = s32[256,1]{1,0:T(8,128)} copy(s32[256,1]{0,1:T(1,128)} %param.11) | data formatting | bytes 2048 | tf_op args[2]
  2.1 102.4 %shard_map.144 = (bf16[256,512]{1,0:T(8,128)(2,1)}, bf16[1,2048,640]{2,1,0:T(8,128)(2,1)}, bf16[1,640,2048]{2,1,0:T(8,128)(2,1)}, f32[1,1024]{1,0:T(1,128)}, f32...) custom-call(bf16[256,2048]{1,0:T(8,128)(2,1)} %tok_hbm.1, bf16[256,2048]{1,0:T(8,128)(2,1)} %grad_hbm.1, ...), custom_call_target="tpu_custom_call" | custom-call | tf_op jit(solution)/shard_map/pallas_call | solution.py:505
  104.5 1.7 %copy.24 = bf16[256,512]{1,0:T(8,128)(2,1)} copy(bf16[256,512]{1,0:T(8,128)(2,1)} %get-tuple-element.14) | data formatting | bytes 524288
  106.2 0.0 copy-start
  106.2 3.6 %copy.25 = bf16[1,2048,640]{2,1,0:T(8,128)(2,1)} copy(bf16[1,2048,640]{2,1,0:T(8,128)(2,1)} %get-tuple-element.15) | data formatting | bytes 5242880
  109.8 0.0 copy-done
  109.8 0.0 copy-start.2
  109.8 0.0 copy-start.4
  109.8 0.0 copy-start.3
  109.8 0.0 copy-start.1
  109.8 1.5 %copy.26 = bf16[1,640,2048]{2,1,0:T(8,128)(2,1)} copy(bf16[1,640,2048]{2,1,0:T(8,128)(2,1)S(1)} %copy-done) | data formatting | bytes 5242880
  111.3 0.0 copy-done.2
  111.3 0.6 copy.27
  111.9 0.0 copy-done.4
  111.9 0.6 copy.28
  112.5 0.0 copy-done.3
  112.5 0.6 copy.29
  113.1 0.0 copy-done.1
  113.1 0.6 copy.30
Async XLA Ops:
  106.2 3.6 %copy-start = (bf16[1,640,2048]{2,1,0:T(8,128)(2,1)S(1)}, bf16[1,640,2048]{2,1,0:T(8,128)(2,1)}, u32[]{:S(2)}) copy-start(bf16[1,640,2048]{2,1,0:T(8,128)(2,1)} %get-tuple-element.16) | copy-start | bytes 7864324
  109.8 1.5 %copy-start.2 = (f32[1,1024]{1,0:T(1,128)S(1)}, f32[1,1024]{1,0:T(1,128)}, u32[]{:S(2)}) copy-start(f32[1,1024]{1,0:T(1,128)} %get-tuple-element.17) | copy-start | bytes 12292
  109.8 2.1 %copy-start.4 = (f32[1,640]{1,0:T(1,128)S(1)}, f32[1,640]{1,0:T(1,128)}, u32[]{:S(2)}) copy-start(f32[1,640]{1,0:T(1,128)} %get-tuple-element.18) | copy-start | bytes 7684
  109.8 2.7 %copy-start.3 = (f32[1,640]{1,0:T(1,128)S(1)}, f32[1,640]{1,0:T(1,128)}, u32[]{:S(2)}) copy-start(f32[1,640]{1,0:T(1,128)} %get-tuple-element.19) | copy-start | bytes 7684
  109.8 3.3 %copy-start.1 = (f32[1,1024]{1,0:T(1,128)S(1)}, f32[1,1024]{1,0:T(1,128)}, u32[]{:S(2)}) copy-start(f32[1,1024]{1,0:T(1,128)} %get-tuple-element.20) | copy-start | bytes 12292

commit v2 on v1

--- a/solution.py
+++ b/solution.py
@@ -22,13 +22,26 @@
     return lax.dot_general(left, right, (contract, ((), ())), preferred_element_type=F32)
 
 
+def plan_of(chunks):
+    if chunks == 2:
+        body = [(["D0"], ["C1"], ["20"]), (["D1"], ["30 40"], ["21"])]
+        return ["S1 A0 B0", "A1 C0 B1"], body, (["31"], ["41"])
+    body = [
+        (["D0"], ["C1 A3 B2"], ["20"]),
+        (["D1"], ["B3 C2 30"], ["C3 21"]),
+        (["D2"], ["40 31"], ["22"]),
+        (["D3"], ["41 32"], ["23"]),
+    ]
+    return ["S1 A0 B0", "S2 A1 C0", "B1 A2 S3"], body, (["33 42"], ["43"])
+
+
 def kernel(
     sizes,
     tok_hbm, grad_hbm, ids_ref, w_hbm, v_hbm, irm_ref, icm_ref, orm_ref, ocm_ref,
     tg_ref, wn_hbm, vn_hbm, irn_ref, icn_ref, orn_ref, ocn_ref,
-    tokq, gradq, place, packed, buf, w_v, v_v, g_in, g_out, pre_s, up_s, act_s, pg_s,
-    tkeep, tsend, trecv, sown, d2s, d2r, nbs, nbr, fin, rbuf, pbuf, nbuf, rs_in, rs_out, a_in, a_out,
-    load_sem, a2a_ss, a2a_rs, x1_ss, x1_rs, x2_ss, x2_rs, cf_ss, cf_rs, tc_ss, tc_rs,
+    tok_v, place, packed, packed_row, buf, w_v, v_v, g_in, g_out, pre_s, up_s, act_s, pg_s,
+    tkeep, tsend, trecv, sown, d2s, d2r, nbs, nbr, fin, rbuf, mom_s, mom_r, pbuf, nbuf, rs_out, a_in, a_out,
+    load_sem, own_sem, mom_ss, mom_rs, a2a_ss, a2a_rs, row_ss, row_rs, cfr_ss, cfr_rs, x1_ss, x1_rs, x2_ss, x2_rs, cf_ss, cf_rs, tc_ss, tc_rs,
     d2_ss, d2_rs, nb_ss, nb_rs, ret_ss, ret_rs, st1_ss, st1_rs, st2_ss, st2_rs, out_sem,
 ):
     T, D, H, Z, Y = sizes
@@ -57,8 +70,10 @@
     def expert_at(dz, dy):
         return ((z + dz + Z) % Z) * Y + (y + dy + Y) % Y
 
+    last = NCH - 1
+
     def dz_of(ch, jj):
-        return -ch if jj == 0 else ch + 1
+        return ch + 1 if jj == 0 else -(ch + 1) * (1 - (ch + 1) // NCH)
 
     def rows(cr, jj):
         return pl.ds(cr * RK + jj * RG, RG)
@@ -74,6 +89,23 @@
             a2a_ss.at[2 * ch + jj, dy], a2a_rs.at[2 * ch + jj, dy], (2 * to + c, x),
         )
 
+    def own_row(dy):
+        to = (y + dy) % Y
+        return remote(
+            packed_row.at[:, :, slots(to), :],
+            buf.at[:, last, :, pl.ds(RG + dy * CAP, CAP), :],
+            row_ss.at[dy], row_rs.at[dy], (2 * (z * Y + to) + c, x),
+        )
+
+    def cf_row():
+        return remote(
+            buf.at[:, last, :, rows(0, 1), :], buf.at[:, last, :, rows(1, 1), :],
+            cfr_ss.at[0], cfr_rs.at[0], core,
+        )
+
+    def mom():
+        return remote(mom_s, mom_r, mom_ss.at[0], mom_rs.at[0], core)
+
     def x1(ch, jj, way, q):
         here = buf.at[q, ch, :, rows(0, jj), :]
         return remote(
@@ -124,13 +156,16 @@
         to = (2 * ((k + off) % K) + c, x)
         return remote(nbuf.at[slot], nbuf.at[slot], st2_ss.at[off], st2_rs.at[off], to)
 
-    columns = pl.ds(pl.multiple_of(x * DQ, DQ), DQ)
-    loads = [
-        pltpu.make_async_copy(tok_hbm.at[:, columns], tokq, load_sem.at[0]),
-        pltpu.make_async_copy(grad_hbm.at[:, columns], gradq, load_sem.at[1]),
-        pltpu.make_async_copy(w_hbm.at[0], w_v, load_sem.at[2]),
-        pltpu.make_async_copy(v_hbm.at[0], v_v, load_sem.at[3]),
-    ]
+    loads = []
+    for a, whole in enumerate((tok_hbm, grad_hbm)):
+        for q in range(4):
+            loads.append(
+                pltpu.make_async_copy(
+                    whole.at[:, pl.ds(q * DQ, DQ)], tok_v.at[a, q], load_sem.at[4 * a + q]
+                )
+            )
+    loads.append(pltpu.make_async_copy(w_hbm.at[0], w_v, load_sem.at[8]))
+    loads.append(pltpu.make_async_copy(v_hbm.at[0], v_v, load_sem.at[9]))
     for load in loads:
         load.start()
     barrier = pltpu.get_barrier_semaphore()
@@ -145,42 +180,70 @@
         )
 
     lanes = max(128, K)
-    chosen = ids_ref[...]
-    onehot = jnp.where(lax.broadcasted_iota(jnp.int32, (T, lanes), 1) == chosen, 1.0, 0.0)
+    chosen = jnp.broadcast_to(ids_ref[...].astype(F32), (128, T)).T[:, :1]
+    onehot = jnp.where(
+        lax.broadcasted_iota(jnp.int32, (T, lanes), 1).astype(F32) == chosen, 1.0, 0.0
+    )
     below = jnp.where(
         lax.broadcasted_iota(jnp.int32, (T, T), 0) > lax.broadcasted_iota(jnp.int32, (T, T), 1), 1.0, 0.0
     )
     earlier = dot(below.astype(BF16), onehot.astype(BF16), ((1,), (0,)))
     rank = jnp.sum(earlier * onehot, axis=1, keepdims=True)
-    slot = chosen * CAP + rank.astype(jnp.int32)
+    slot = (chosen * CAP + rank).astype(jnp.int32)
     place[...] = jnp.where(
         lax.broadcasted_iota(jnp.int32, (T, K * CAP), 1) == slot, 1.0, 0.0
     ).astype(BF16)
-    loads[0].wait()
-    packed[0] = dot(place[...], tokq[...], ((0,), (0,))).astype(BF16)
-    loads[1].wait()
-    packed[1] = dot(place[...], gradq[...], ((0,), (0,))).astype(BF16)
+    for load in loads[:8]:
+        load.wait()
+    for a in range(2):
+        packed[a] = dot(place[...], tok_v[a, x], ((0,), (0,))).astype(BF16)
+    mom_s[:, :DH] = irm_ref[...]
+    mom_s[:, DH:] = ocm_ref[...]
     pl.semaphore_wait(barrier, K - 1 + len(column_peers))
 
-    every = [(ch, jj, dy) for ch in range(NCH) for jj in range(2) for dy in range(Y)][1:]
-    for ch, jj, dy in every:
-        a2a(ch, jj, dy).start()
+    halves = [(ch, jj) for ch in range(NCH) for jj in range(2)][:-1]
+    away = [(ch, jj, dy) for ch, jj in halves for dy in range(Y)]
+    row_peers = range(1, Y)
+
+    def send(ch, jj):
+        for dy in range(Y):
+            a2a(ch, jj, dy).start()
+
+    def sent(ch, jj):
+        for dy in range(Y):
+            a2a(ch, jj, dy).wait_send()
+
+    send(0, 0)
+    send(0, 1)
+    mom().start()
+    row_lanes = max(128, RG)
+    row_place = jnp.where(
+        lax.broadcasted_iota(jnp.int32, (T, row_lanes), 1) + z * RG == slot, 1.0, 0.0
+    ).astype(BF16)
+    for q in range(4):
+        for a in range(2):
+            packed_row[q, a] = dot(row_place, tok_v[a, q], ((0,), (0,)))[:RG].astype(BF16)
+    for dy in row_peers:
+        own_row(dy).start()
     own = pltpu.make_async_copy(
-        packed.at[:, slots(k), :], buf.at[x, 0, :, pl.ds(0, CAP), :], load_sem.at[4]
+        packed_row.at[:, :, slots(y), :], buf.at[:, last, :, pl.ds(RG, CAP), :], own_sem.at[0]
     )
     own.start()
     g_in[...] = jnp.zeros_like(g_in)
     g_out[...] = jnp.zeros_like(g_out)
 
-    def step_a(ch, jj, first=False):
+    def step_a(ch, jj):
         for dy in range(Y):
-            if first and dy == 0:
-                own.wait()
-            else:
-                a2a(ch, jj, dy).wait_recv()
+            a2a(ch, jj, dy).wait_recv()
         x1(ch, jj, 0, x).start()
         x1(ch, jj, 1, x).start()
         cf(ch, jj, 0).start()
+
+    def step_a_row():
+        own.wait()
+        for dy in row_peers:
+            own_row(dy).wait_recv()
+        cf_row().start()
 
     def step_b(ch, jj):
         x1(ch, jj, 0, xl).wait_recv()
@@ -195,10 +258,12 @@
         x2(ch, jj, 1, xo).wait_recv()
         cf(ch, jj, 2).start()
 
-    def step_d(ch):
-        for jj in range(2):
-            for rq in range(4):
-                cf(ch, jj, rq).wait_recv()
+    def step_d(ch, jj):
+        for rq in range(4):
+            cf(ch, jj, rq).wait_recv()
+
+    def step_d_row():
+        cf_row().wait_recv()
 
     def forward(ch):
         for q in range(4):
@@ -226,7 +291,7 @@
             part = slice(q * DQ, (q + 1) * DQ)
             t = dot(pg_s[...], w_v[part, :], ((1,), (1,)))
             tsend[ch, q] = t[RK:].astype(BF16)
-            tkeep[q] = t[:RK]
+            tkeep[ch, q] = t[:RK]
         tc(ch).start()
 
     def grads_in(ch):
@@ -241,21 +306,21 @@
 
     def step_r2(ch):
         tc(ch).wait_recv()
-        both = tkeep[xo] + trecv[ch, xo].astype(F32)
+        both = tkeep[ch, xo] + trecv[ch, xo].astype(F32)
         d2s[ch, 0] = both[:RG].astype(BF16)
         d2s[ch, 1] = both[RG:].astype(BF16)
         d2(ch, 0).start()
         d2(ch, 1).start()
-        sown[ch] = tkeep[x] + trecv[ch, x].astype(F32)
+        sown[ch] = tkeep[ch, x] + trecv[ch, x].astype(F32)
 
     def step_r3(ch):
         d2(ch, 0).wait_recv()
-        to_right = tkeep[xr] + trecv[ch, xr].astype(F32)
+        to_right = tkeep[ch, xr] + trecv[ch, xr].astype(F32)
         nbs[ch, 0, :RG] = (to_right[:RG] + d2r[ch, 0].astype(F32)).astype(BF16)
         nbs[ch, 0, RG:] = to_right[RG:].astype(BF16)
         nb(ch, 0).start()
         d2(ch, 1).wait_recv()
-        to_left = tkeep[xl] + trecv[ch, xl].astype(F32)
+        to_left = tkeep[ch, xl] + trecv[ch, xl].astype(F32)
         nbs[ch, 1, :RG] = to_left[:RG].astype(BF16)
         nbs[ch, 1, RG:] = (to_left[RG:] + d2r[ch, 1].astype(F32)).astype(BF16)
         nb(ch, 1).start()
@@ -266,50 +331,70 @@
         fin[ch] = (sown[ch] + nbr[ch, 0].astype(F32) + nbr[ch, 1].astype(F32)).astype(BF16)
         for jj in range(2):
             for dy in range(Y):
-                if jj or dy:
+                if dy or not jj:
                     ret(ch, jj, dy, k).start()
 
-        @pl.when(ch > 0)
-        def _():
-            ret(ch, 0, 0, k).start()
-
-        @pl.when(ch == 0)
-        def _():
-            rbuf[slots(k), :] = fin[0, :CAP, :]
-
-    def also(condition, *steps):
-        @pl.when(condition)
-        def _():
-            for function, *args in steps:
-                function(*args)
-
-    step_a(0, 0, first=True)
-    step_a(0, 1)
-    step_b(0, 0)
-    step_a(1, 0)
-    step_b(0, 1)
-    step_c(0, 0)
-    step_a(1, 1)
-    step_b(1, 0)
-    step_c(0, 1)
-    loads[2].wait()
-    loads[3].wait()
+        if ch < last:
+            ret(ch, 1, 0, k).start()
+        else:
+            rbuf[slots(k), :] = fin[last, RG : RG + CAP, :]
+
+    def stage(n, step, row_step=None):
+        if 0 <= n < NCH:
+            step(n, 0)
+        if 0 <= n < last:
+            step(n, 1)
+        if n == last and row_step is not None:
+            row_step()
+
+    def send_after(n):
+        stage(n - 1, sent)
+        stage(n, send)
+
+    def later(n, step):
+        if 0 <= n < NCH:
+            step(n)
+
+    def act(name, n):
+        if name == "S":
+            send_after(n)
+        elif name == "A":
+            stage(n, step_a, step_a_row)
+        elif name == "B":
+            stage(n, step_b)
+        elif name == "C":
+            stage(n, step_c)
+        elif name == "D":
+            stage(n, step_d, step_d_row)
+        else:
+            later(n, {"2": step_r2, "3": step_r3, "4": step_r4}[name])
+
+    def run(plan):
+        for word in " ".join(plan).split():
+            act(word[0], int(word[1:]))
+
+    before, body, after = plan_of(NCH)
+    run(before)
+    loads[8].wait()
+    loads[9].wait()
+
+    def during(ch, part):
+        for n, parts in enumerate(body):
+            if parts[part]:
+                pl.when(ch == n)(functools.partial(run, parts[part]))
 
     def chunk(ch, carry):
-        also(ch + 2 < NCH, (step_a, ch + 2, 0))
-        also(ch + 1 < NCH, (step_b, ch + 1, 1), (step_c, ch + 1, 0))
-        step_d(ch)
+        during(ch, 0)
         forward(ch)
-        also(ch > 0, (step_r4, ch - 1))
-        also(ch + 2 < NCH, (step_a, ch + 2, 1), (step_b, ch + 2, 0))
+        during(ch, 1)
         grads_in(ch)
-        step_r2(ch)
-        also(ch + 1 < NCH, (step_c, ch + 1, 1))
         grads_out(ch)
-        step_r3(ch)
+        during(ch, 2)
         return carry
 
     lax.fori_loop(0, NCH, chunk, 0)
+
+    mine = x * 2 + c
 
     def squares_in(i, total):
         some = pl.ds(pl.multiple_of(i * 128, 128), 128)
@@ -318,7 +403,7 @@
         narrow = s[:, :128]
         for t in range(1, H // 128):
             narrow = narrow + s[:, t * 128 : (t + 1) * 128]
-        rs_in[:, some] = jnp.sum(narrow.T, axis=0, keepdims=True)
+        pbuf[mine, :, some] = jnp.sum(narrow.T, axis=0, keepdims=True)
         return total + jnp.sum(s.reshape(16, 8, H), axis=0)
 
     def squares_out(i, total):
@@ -341,43 +426,35 @@
     def total_of(row):
         return jnp.sum(row, axis=1, keepdims=True)
 
-    mine = x * 2 + c
-    norm_part = total_of(cs_in) + total_of(cs_out)
-    pbuf[mine, 0:1] = rs_in[:, :DH]
-    pbuf[mine, 1:2] = rs_in[:, DH:]
-    pbuf[mine, 2:3] = cs_out[:, :DH]
-    pbuf[mine, 3:4] = cs_out[:, DH:]
-    pbuf[mine, 4:5] = irm_ref[...]
-    pbuf[mine, 5:6] = ocm_ref[...]
-    pbuf[mine, 6:7] = jnp.broadcast_to(norm_part, (1, DH))
-    pbuf[mine, 7:8, : DH // 2] = jnp.broadcast_to(total_of(orm_ref[...]), (1, DH // 2))
-    pbuf[mine, 7:8, DH // 2 :] = jnp.broadcast_to(total_of(rs_out[...]), (1, DH // 2))
+    pbuf[mine, :, D : 2 * D] = cs_out
+    scalars = (total_of(cs_in) + total_of(cs_out), total_of(orm_ref[...]), total_of(rs_out[...]))
+    for i, scalar in enumerate(scalars):
+        pbuf[mine, :, 2 * D + i * 128 : 2 * D + (i + 1) * 128] = jnp.broadcast_to(scalar, (1, 128))
     for dx, dc in column_peers:
         st1(dx, dc, mine).start()
-    step_r4(NCH - 1)
+    run(after[0])
     for dx, dc in column_peers:
         st1(dx, dc, ((x - dx + 4) % 4) * 2 + (c + dc) % 2).wait_recv()
     sums = pbuf[0]
     for s in range(1, 8):
         sums = sums + pbuf[s]
-    nbuf[k] = jnp.broadcast_to(sums[6:7, :128], (8, 128))
+    nbuf[k] = sums[:, 2 * D : 2 * D + 128]
     for off in range(1, K):
         st2(off, k).start()
-
-    for ch, jj, dy in every:
-        ret(ch, jj, dy, expert_at(dz_of(ch, jj), dy)).wait_recv()
-    tg_ref[...] = dot(place[...], rbuf[...], ((1,), (0,))).astype(BF16)
+    run(after[1])
 
     for off in range(1, K):
         st2(off, (k - off + K) % K).wait_recv()
     norm_total = jnp.sum(nbuf[...], axis=0)[0:1, 0:1]
     clip = jnp.minimum(1.0, jnp.sqrt((2.0 * K * D * FF) / norm_total))
     clip_two = clip * clip
-    zero, one = pbuf[x * 2], pbuf[x * 2 + 1]
-    old_in_row = jnp.concatenate([zero[4:5], one[4:5]], axis=1)
-    old_out_col = jnp.concatenate([zero[5:6], one[5:6]], axis=1)
-    row_in = jnp.concatenate([sums[0:1], sums[1:2]], axis=1)
-    col_out = jnp.concatenate([sums[2:3], sums[3:4]], axis=1)
+    mom().wait_recv()
+    mom_own, mom_other = mom_s[...], mom_r[...]
+    mom_zero = jnp.where(c == 0, mom_own, mom_other)
+    mom_one = jnp.where(c == 0, mom_other, mom_own)
+    old_in_row = jnp.concatenate([mom_zero[:, :DH], mom_one[:, :DH]], axis=1)
+    old_out_col = jnp.concatenate([mom_zero[:, DH:], mom_one[:, DH:]], axis=1)
+    row_in, col_out = sums[:, :D], sums[:, D : 2 * D]
 
     def moved(old, squares, count):
         return beta_two * old + (1.0 - beta_two) * (clip_two * (squares / count) + epsilon_one)
@@ -387,7 +464,7 @@
     out_row = moved(orm_ref[...], rs_out[...], D)
     out_col = moved(old_out_col, col_out, FF)
     mean_in = total_of(in_row) / D
-    mean_out = moved(sums[7:8, 0:1] / FF, sums[7:8, DH // 2 : DH // 2 + 1] / D, FF)
+    mean_out = moved(sums[:, 2 * D + 128 : 2 * D + 129] / FF, sums[:, 2 * D + 256 : 2 * D + 257] / D, FF)
     irn_ref[...] = jnp.where(c == 0, in_row[:, :DH], in_row[:, DH:])
     ocn_ref[...] = jnp.where(c == 0, out_col[:, :DH], out_col[:, DH:])
     icn_ref[...] = in_col
@@ -423,26 +500,49 @@
         outs.append(pltpu.make_async_copy(v_v.at[part, :], vn_hbm.at[0, part, :], out_sem.at[4 + i]))
         outs[-1].start()
 
-    for ch, jj, dy in every:
-        a2a(ch, jj, dy).wait_send()
+    back = away + [(last, 1, dy) for dy in row_peers]
+    for ch, jj, dy in back:
+        ret(ch, jj, dy, expert_at(dz_of(ch, jj), dy)).wait_recv()
+    tg_ref[...] = dot(place[...], rbuf[...], ((1,), (0,))).astype(BF16)
+
+    stage(last, sent)
+    mom().wait_send()
+    cf_row().wait_send()
+    for ch, jj, dy in back:
         ret(ch, jj, dy, k).wait_send()
+    for dy in row_peers:
+        own_row(dy).wait_send()
     for ch in range(NCH):
         tc(ch).wait_send()
         for way in range(2):
             d2(ch, way).wait_send()
             nb(ch, way).wait_send()
-            for jj in range(2):
-                x1(ch, jj, way, x).wait_send()
-                x2(ch, jj, way, (xl, xr)[way]).wait_send()
-        for jj in range(2):
-            for rq in range(4):
-                cf(ch, jj, rq).wait_send()
+    for ch, jj in halves:
+        for way in range(2):
+            x1(ch, jj, way, x).wait_send()
+            x2(ch, jj, way, (xl, xr)[way]).wait_send()
+        for rq in range(4):
+            cf(ch, jj, rq).wait_send()
     for dx, dc in column_peers:
         st1(dx, dc, mine).wait_send()
     for off in range(1, K):
         st2(off, k).wait_send()
     for out in outs:
         out.wait()
+
+
+def deliver(*refs):
+    sem = refs[14]
+    copies = []
+    for i, (src, dst) in enumerate(zip(refs[:7], refs[7:14])):
+        cuts = 4 if i in (1, 2) else 1
+        size = src.shape[1] // cuts
+        for part in range(cuts):
+            at = (slice(None), pl.ds(part * size, size)) if cuts > 1 else (slice(None),) * 2
+            copies.append(pltpu.make_async_copy(src.at[at], dst.at[at], sem.at[len(copies)]))
+            copies[-1].start()
+    for copy in copies:
+        copy.wait()
 
 
 def shards(
@@ -460,10 +560,10 @@
     vmem = pl.BlockSpec(memory_space=pltpu.VMEM)
     dma = pltpu.SemaphoreType.DMA
     scratch = [
-        pltpu.VMEM((T, DQ), BF16),
-        pltpu.VMEM((T, DQ), BF16),
+        pltpu.VMEM((2, 4, T, DQ), BF16),
         pltpu.VMEM((T, K * CAP), BF16),
         pltpu.VMEM((2, K * CAP, DQ), BF16),
+        pltpu.VMEM((4, 2, RG, DQ), BF16),
         pltpu.VMEM((4, NCH, 2, R, DQ), BF16),
         pltpu.VMEM((D, H), BF16),
         pltpu.VMEM((H, D), BF16),
@@ -473,7 +573,7 @@
         pltpu.VMEM((R, H), F32),
         pltpu.VMEM((R, H), BF16),
         pltpu.VMEM((R, H), BF16),
-        pltpu.VMEM((4, RK, DQ), F32),
+        pltpu.VMEM((NCH, 4, RK, DQ), F32),
         pltpu.VMEM((NCH, 4, RK, DQ), BF16),
         pltpu.VMEM((NCH, 4, RK, DQ), BF16),
         pltpu.VMEM((NCH, RK, DQ), F32),
@@ -483,14 +583,18 @@
         pltpu.VMEM((NCH, 2, RK, DQ), BF16),
         pltpu.VMEM((NCH, RK, DQ), BF16),
         pltpu.VMEM((K * CAP, DQ), BF16),
-        pltpu.VMEM((8, 8, D // 2), F32),
-        pltpu.VMEM((K, 8, 128), F32),
         pltpu.VMEM((1, D), F32),
+        pltpu.VMEM((1, D), F32),
+        pltpu.VMEM((8, 1, 2 * D + 3 * 128), F32),
+        pltpu.VMEM((K, 1, 128), F32),
         pltpu.VMEM((1, H), F32),
         pltpu.VMEM((1, D), F32),
         pltpu.VMEM((1, H), F32),
-        dma((5,)),
+        dma((10,)), dma((1,)),
+        dma((1,)), dma((1,)),
         dma((Z, Y)), dma((Z, Y)),
+        dma((Y,)), dma((Y,)),
+        dma((1,)), dma((1,)),
         dma((Z, 2)), dma((Z, 2)),
         dma((Z, 2)), dma((Z, 2)),
         dma((Z, 4)), dma((Z, 4)),
@@ -502,24 +606,38 @@
         dma((K,)), dma((K,)),
         dma((4 + H // 128,)),
     ]
-    return pl.pallas_call(
+    results = pl.pallas_call(
         functools.partial(kernel, (T, D, H, Z, Y)),
-        out_shape=(
-            jax.ShapeDtypeStruct((T, DQ), BF16),
-            jax.ShapeDtypeStruct(w_in.shape, BF16),
-            jax.ShapeDtypeStruct(w_out.shape, BF16),
-            jax.ShapeDtypeStruct(in_row_mom.shape, F32),
-            jax.ShapeDtypeStruct(in_col_mom.shape, F32),
-            jax.ShapeDtypeStruct(out_row_mom.shape, F32),
-            jax.ShapeDtypeStruct(out_col_mom.shape, F32),
+        out_shape=tuple(
+            pltpu.VMEM(shape, dtype)
+            for shape, dtype in (
+                ((T, DQ), BF16),
+                (w_in.shape, BF16),
+                (w_out.shape, BF16),
+                (in_row_mom.shape, F32),
+                (in_col_mom.shape, F32),
+                (out_row_mom.shape, F32),
+                (out_col_mom.shape, F32),
+            )
         ),
         in_specs=[hbm, hbm, vmem, hbm, hbm, vmem, vmem, vmem, vmem],
         out_specs=(vmem, hbm, hbm, vmem, vmem, vmem, vmem),
         scratch_shapes=scratch,
         compiler_params=pltpu.CompilerParams(
-            collective_id=0, has_side_effects=True, vmem_limit_bytes=56 * 1024 * 1024
+            collective_id=0, has_side_effects=True, vmem_limit_bytes=52 * 1024 * 1024
         ),
-    )(tokens, out_grad, expert_ids, w_in, w_out, in_row_mom, in_col_mom, out_row_mom, out_col_mom)
+    )(
+        tokens, out_grad, expert_ids.reshape(1, T), w_in, w_out,
+        in_row_mom, in_col_mom, out_row_mom, out_col_mom,
+    )
+    return pl.pallas_call(
+        deliver,
+        out_shape=tuple(jax.ShapeDtypeStruct(r.shape, r.dtype) for r in results),
+        in_specs=[hbm] * 7,
+        out_specs=(hbm,) * 7,
+        scratch_shapes=[dma((13,))],
+        compiler_params=pltpu.CompilerParams(vmem_limit_bytes=1024 * 1024),
+    )(*results)
 
 
 def solution(mesh):

time: 115 us -> 92.2 us (0.80)
  Pallas kernels: 102 us -> 89.9 us
  local copies, waits for them, and re-layouts: 10.6 us -> 0 us
    pallas_call x1 -> x2, Pallas kernels: 102 us -> 89.9 us  [the longest x1 87.4 us: shards(): pl.pallas_call(functools.partial(kernel, (T, D, H, Z, Y)), out_shape=tupl...]
    unnamed x18 -> x0, local copies, waits for them, and re-layouts: 10.6 us -> none
where the time goes in v2:
time: 92.2 us; the launch traced here: 90.6 us
  Pallas kernels  89.9 us (98%)
    pallas_call x1, Pallas kernels, shards(): pl.pallas_call(functools.partial(kernel, (T, D, H, Z, Y)), out_shape=tupl...  87.4 us
    pallas_call x1, Pallas kernels, shards(): pl.pallas_call(deliver, out_shape=tuple((jax.ShapeDtypeStruct(r.shape, r....  2.54 us

profile of v2, /device:TPU:8, one launch (start us, length us, event | category | flops | bytes accessed | tf_op | source)
XLA Modules:
  0.0 90.6 jit_solution(8823631062175780790)
XLA Ops:
  0.6 87.4 %shard_map.144 = (bf16[256,512]{1,0:T(8,128)(2,1)S(1)}, bf16[1,2048,640]{2,1,0:T(8,128)(2,1)S(1)}, bf16[1,640,2048]{2,1,0:T(8,128)(2,1)S(1)}, f32[1,1024]{1,0:T(...) custom-call(bf16[256,2048]{1,0:T(8,128)(2,1)} %tok_hbm.1, ...), custom_call_target="tpu_custom_call" | custom-call | tf_op jit(solution)/shard_map/pallas_call | solution.py:609
  88.0 2.5 %shard_map.145 = (bf16[256,512]{1,0:T(8,128)(2,1)}, bf16[1,2048,640]{2,1,0:T(8,128)(2,1)}, bf16[1,640,2048]{2,1,0:T(8,128)(2,1)}, f32[1,1024]{1,0:T(1,128)}, f32...) custom-call(bf16[256,512]{1,0:T(8,128)(2,1)S(1)} %get-tuple-element.14.refs_0_, ...), custom_call_target="tpu_custom_call" | custom-call | tf_op jit(solution)/shard_map/pallas_call | solution.py:633
